TPU v7x, 32 devices: a whole 2x2x4 slice. The times are simulated.
32 devices in a mesh: rows: 16 (over z, y, x), cols: 2 (over core).
Axes of the slice: x: 2, y: 2, z: 4, core: 2. Of those that a mesh axis runs over, the one named last changes fastest.
Arguments:
- basis_t: bfloat16 [512, 65536], P('cols', 'rows'), may hold values from -0.75 to 0.75
- diag_tiles: bfloat16 [512, 128, 128], P('rows'), may hold values from -0.1875 to 0.1875
- off_tiles: bfloat16 [512, 8, 128, 128], P('rows'), may hold values from -0.1875 to 0.1875
- owners: int32 [512, 8], P('rows'), may hold values from 0 to 15, all different within a row; in each aligned block of 32 rows (0 to 31, 32 to 63, ...) at most 16 rows name the same one
- tile_block: int32 [512, 8], P('rows'), may hold values from 0 to 31
Outputs:
- reduced: float32 [512, 512], P('rows', 'cols')
Inputs may be any that keep to these rules, and one draw needn't show every extreme that they name: Each block row names 8 different owners. Among the 32 block rows of one index of rows, no owner is named by more than 16 of them, a bound that some block reaches.
All inputs are finite; a program needn't handle non-finite values.
Results may differ from a plain program's by a relative error of at most 0.0029.
Values may be sent and summed in bfloat16 or wider, within the bound.
A program may use at most 128 MiB of HBM per device.

v0:
```python
import jax
import jax.numpy as jnp
from jax import lax
from jax.sharding import PartitionSpec as P

BS = 128
TPR = 8


def per_device(basis_t, diag_tiles, off_tiles, owners, tile_block):
    width = basis_t.shape[0]
    local_rows = off_tiles.shape[0]
    row_devices = lax.axis_size("rows")
    local_blocks = basis_t.reshape(width, local_rows, BS)
    flat_owners = owners.reshape(-1)
    flat_blocks = tile_block.reshape(-1)
    whole_basis = lax.all_gather(basis_t, "rows", axis=1, tiled=True)
    all_blocks = whole_basis.reshape(width, row_devices * local_rows, BS)
    tile_panels = all_blocks[:, flat_owners * local_rows + flat_blocks, :]
    tile_panels = tile_panels.reshape(width, local_rows, TPR, BS)
    image = jnp.einsum("cbkj,bkij->cbi", tile_panels, off_tiles, preferred_element_type=jnp.float32)
    image = image + jnp.einsum(
        "cbj,bij->cbi", local_blocks, diag_tiles, preferred_element_type=jnp.float32
    )
    image_t = image.astype(jnp.bfloat16).reshape(width, local_rows * BS)
    partial_sums = lax.dot_general(
        lax.all_gather(basis_t, "cols", axis=0, tiled=True),
        image_t,
        (((1,), (1,)), ((), ())),
        preferred_element_type=jnp.float32,
    )
    return lax.psum_scatter(partial_sums, "rows", scatter_dimension=0, tiled=True)


def solution(mesh):
    in_specs = (
        P("cols", "rows"),
        P("rows", None, None),
        P("rows", None, None, None),
        P("rows", None),
        P("rows", None),
    )
    out_specs = P("rows", "cols")
    return jax.shard_map(
        per_device, mesh=mesh, in_specs=in_specs, out_specs=out_specs, check_vma=False
    )
```

profile of v0, /device:TPU:0, one launch (start us, length us, event | category | flops | bytes accessed | tf_op | source)
XLA Modules:
  0.0 520.9 jit_solution(10012501521852356117)
XLA Ops:
  6.5 0.0 copy-start
  6.5 0.0 copy-start.3
  6.5 0.0 copy-start.2
  6.5 0.0 all-gather.3.cloned.1.call-start
  6.5 4.2 copy.17
  10.7 0.0 all-gather.3.cloned.1.call-update
  10.8 0.0 all-gather.5.cloned.1.call-start
  10.8 0.7 all-gather.5.cloned.1.call-update
  11.5 0.0 reduce-scatter.4.cloned.1.call-start
  11.6 0.0 copy-done.3
  11.6 0.0 copy-done.2
  11.6 0.1 copy.18
  11.7 0.1 add.32
  11.8 352.7 %all-gather.3.cloned.1.call-done = bf16[256,65536]{0,1:T(8,128)(2,1)} async-done(((bf16[256,4096]{0,1:T(8,128)(2,1)}), bf16[256,65536]{0,1:T(8,128)(2,1)}) %all-gather.3.cloned.1.call-update) | async-done | bytes 33554448 | tf_op jit(solution)/shard_map/all_gather | solution.py:17
  364.5 40.5 %copy.19 = bf16[256,512,128]{2,0,1:T(8,128)(2,1)} copy(bf16[256,512,128]{0,2,1:T(8,128)(2,1)} %bitcast.31) | data formatting | bytes 67108864 | tf_op jit(solution)/shard_map/reshape | solution.py:18
  405.0 12.7 %gather_fusion = bf16[256,256,128]{2,1,0:T(8,128)(2,1)} fusion(bf16[256,512,128]{2,0,1:T(8,128)(2,1)} %copy.19, s32[1024]{0:T(1024)S(1)} %pad_clamp_fusion), kind=kCustom, calls=%fused_computation | custom fusion | bytes 33555456 | tf_op jit(solution)/shard_map/gather | solution.py:19
  417.6 10.7 %fusion.3 = f32[32,256,128,1]{1,2,3,0:T(8,128)S(1)} fusion(bf16[256,32,8,128]{3,0,2,1:T(8,128)(2,1)} %bitcast.30, bf16[32,8,128,128]{3,2,1,0:T(8,128)(2,1)} %param.7), kind=kOutput, calls=%fused_computation.9 | convolution fusion | flops 2147483648 | bytes 29360128 | tf_op jit(solution)/shard_map/cbkj,bkij->cbi/dot_general | solution.py:21
  428.4 0.0 copy-done
  428.4 0.0 copy-done.1
  428.4 2.1 fusion
  430.5 4.1 convolution_bitcast_fusion
  434.6 1.0 copy.23
  435.6 0.0 reduce-scatter.4.cloned.1.call-update
  435.6 78.8 %reduce-scatter.4.cloned.1.call-done = f32[32,256]{1,0:T(8,128)} async-done(((f32[512,256]{1,0:T(8,128)}), f32[32,256]{1,0:T(8,128)}) %reduce-scatter.4.cloned.1.call-update) | async-done | bytes 32784 | tf_op jit(solution)/shard_map/reduce_scatter | solution.py:32
  (5 shorter events, 0.0 us)
Async XLA Ops:
  6.5 421.8 %copy-start = (bf16[32,128,128]{2,1,0:T(8,128)(2,1)S(1)}, bf16[32,128,128]{2,1,0:T(8,128)(2,1)}, u32[]{:S(2)}) copy-start(bf16[32,128,128]{2,1,0:T(8,128)(2,1)} %param.6) | copy-start | bytes 3145732
  6.5 5.0 copy-start.3
  6.5 5.0 copy-start.2
  6.5 357.9 %all-gather.3.cloned.1.call-start = ((), (), s32[]{:S(2)}) async-start(), calls=%async_computation.1 | async-start | bytes 35651584 | tf_op jit(solution)/shard_map/all_gather | solution.py:17
  10.8 419.7 %all-gather.5.cloned.1.call-start = ((), (), s32[]{:S(2)}) async-start(), calls=%async_computation.2 | async-start | bytes 6291456 | tf_op jit(solution)/shard_map/all_gather | solution.py:27
  11.5 502.9 %reduce-scatter.4.cloned.1.call-start = ((), (), s32[]{:S(2)}) async-start(), calls=%async_computation.3 | async-start | bytes 557056 | tf_op jit(solution)/shard_map/reduce_scatter | solution.py:32
  417.6 10.7 %copy-start.1 = (bf16[256,4096]{1,0:T(8,128)(2,1)S(1)}, bf16[256,4096]{1,0:T(8,128)(2,1)}, u32[]{:S(2)}) copy-start(bf16[256,4096]{1,0:T(8,128)(2,1)} %param.5) | copy-start | bytes 6291460
Sparse Core Ops, SparseCore 0:
  10.9 353.5 all-gather.2
  366.0 11.8 all-gather.4
  435.7 78.5 reduce-scatter.3
where the time goes:
time: 522 us; the launch traced here: 521 us
  waiting for transfers between devices  432 us (83%)
  local copies, waits for them, and re-layouts  58.5 us (11%)
  matrix products  16.9 us (3%)
  between operations  13.2 us (3%)
    all_gather x1, waiting for transfers between devices, per_device(): whole_basis = lax.all_gather(basis_t, 'rows', axis=1, tiled=True)  353 us
    reduce_scatter x1, waiting for transfers between devices, per_device(): lax.psum_scatter(partial_sums, 'rows', scatter_dimension=0, tiled=True)  78.8 us
    reshape x1, local copies, waits for them, and re-layouts, per_device(): all_blocks = whole_basis.reshape(width, row_devices * local_rows, BS)  40.5 us
    gather x1, local copies, waits for them, and re-layouts, per_device(): tile_panels = all_blocks[:, flat_owners * local_rows + flat_blocks, :]  12.7 us
    dot_general x1, matrix products, per_device(): jnp.einsum('cbkj,bkij->cbi', tile_panels, off_tiles, preferred_element_ty...  10.7 us
  transfers between devices with their start and end apart: 3, of which 2 were waited for; matrix products, arithmetic and copies ran while one was open for 13% of the time, Pallas kernels for 0%

commit v1 on v0

v1 whole, which is shorter than its diff:
```python
import functools

import jax
import jax.numpy as jnp
from jax import lax
from jax.experimental import pallas as pl
from jax.experimental.pallas import tpu as pltpu
from jax.sharding import PartitionSpec as P

BS = 128
TPR = 8
PIECES = 4
MESH = pl.DeviceIdType.MESH
NT = (((1,), (1,)), ((), ()))
MIB = 1 << 20


def gather_kernel(
    n_rows, basis, off, diag, own, tile, vall, offp, diagp, ownp, tilep, pv, local_sem, send, recv, isend, irecv
):
    r, c = lax.axis_index("rows"), lax.axis_index("cols")
    x, y = r % 2, (r // 2) % 2
    width, nodes = basis.shape
    slab = width // 2
    rounds = 2 * PIECES
    piece = slab // PIECES
    rest = width // rounds
    half_rows = off.shape[0] // 2
    step_rows = half_rows // rounds
    lines = n_rows // 4
    side = r + 1 - 2 * x
    across = r + 2 - 4 * y
    twin = 1 - c
    z_kinds, y_kinds = lines - 1, lines
    Y0 = z_kinds
    XV = Y0 + y_kinds
    XA, XB, XD, CA, CB, CD, CO = range(XV + 1, XV + 8)

    barrier = pltpu.get_barrier_semaphore()
    friends = [(side, c), (across, c), (r, twin)] + [((r + 4 * d) % n_rows, c) for d in range(1, lines)]
    for friend in friends:
        pl.semaphore_signal(barrier, inc=1, device_id=friend, device_id_type=MESH)
    pl.semaphore_wait(barrier, len(friends))

    def copy(s, kind, src, dst, device):
        return pltpu.make_async_remote_copy(
            src_ref=src, dst_ref=dst, send_sem=send.at[s, kind], recv_sem=recv.at[s, kind],
            device_id=device, device_id_type=MESH,
        )

    def part(home, d, s):
        origin = (home - 4 * d + n_rows) % n_rows + (s // PIECES) * (1 - 2 * x)
        return vall.at[origin, pl.ds(pl.multiple_of((s % PIECES) * piece, piece), piece), :]

    def z_send(d, s):
        here = part(r, 0, s)
        return copy(s, d - 1, here, here, ((r + 4 * d) % n_rows, c))

    def z_recv(d, s):
        there = part(r, d, s)
        return copy(s, d - 1, there, there, (side, c))

    def y_send(d, s):
        here = part(r, d, s)
        return copy(s, Y0 + d, here, here, (across, c))

    def y_recv(d, s):
        there = part(across, d, s)
        return copy(s, Y0 + d, there, there, (across, c))

    def xv_send(s):
        rows = pl.multiple_of(s * piece, piece)
        src = basis.at[pl.ds(pl.multiple_of((1 - x) * slab + rows, piece), piece), :]
        return copy(s, XV, src, vall.at[r, pl.ds(rows, piece), :], (side, c))

    def xv_recv(s):
        dst = vall.at[side, pl.ds(pl.multiple_of(s * piece, piece), piece), :]
        return copy(s, XV, dst, dst, (side, c))

    def tiles(ref, core, s):
        return ref.at[pl.ds(core * half_rows + s * step_rows, step_rows)]

    def band(ref, s):
        return ref.at[pl.ds(pl.multiple_of(s * rest, rest), rest), :]

    def x_rest(s):
        return [
            copy(s, XA, tiles(off, c, s), tiles(offp, c, s), (side, c)),
            copy(s, XB, band(basis, s), band(pv.at[1], s), (side, c)),
            copy(s, XD, tiles(diag, c, s), tiles(diagp, c, s), (side, c)),
        ]

    def c_rest(s):
        return [
            copy(s, CA, tiles(offp, c, s), tiles(offp, c, s), (r, twin)),
            copy(s, CB, band(pv.at[1], s), band(pv.at[2], s), (r, twin)),
            copy(s, CD, tiles(diagp, c, s), tiles(diagp, c, s), (r, twin)),
        ]

    def c_recv(s):
        return [
            copy(s, CA, tiles(offp, twin, s), tiles(offp, twin, s), (r, twin)),
            copy(s, CB, band(pv.at[2], s), band(pv.at[2], s), (r, twin)),
            copy(s, CD, tiles(diagp, twin, s), tiles(diagp, twin, s), (r, twin)),
        ]

    def c_own(s):
        return copy(s, CO, band(basis, s), band(pv.at[0], s), (r, twin))

    keep = pltpu.make_async_copy(basis.at[pl.ds(pl.multiple_of(x * slab, slab), slab), :], vall.at[r], local_sem)
    keep.start()
    listed = [
        pltpu.make_async_remote_copy(
            src_ref=a, dst_ref=b, send_sem=isend.at[i], recv_sem=irecv.at[i], device_id=(side, c), device_id_type=MESH
        )
        for i, (a, b) in enumerate(((own, ownp), (tile, tilep)))
    ]
    for one in listed:
        one.start()
    keep.wait()

    def pass_on(s):
        for d in range(1, lines):
            z_recv(d, s).wait_recv()
            y_send(d, s).start()
        for came, go in zip(x_rest(s), c_rest(s)):
            came.wait_recv()
            go.start()

    @pl.loop(0, rounds)
    def _(s):
        @pl.when(s < PIECES)
        def _():
            xv_send(s).start()

        @pl.when(s >= PIECES)
        def _():
            xv_recv(s - PIECES).wait_recv()

        for d in range(1, lines):
            z_send(d, s).start()
        y_send(0, s).start()
        for one in x_rest(s):
            one.start()
        c_own(s).start()

        @pl.when(s >= 1)
        def _():
            pass_on(s - 1)

    pass_on(rounds - 1)

    @pl.loop(0, rounds)
    def _(s):
        for d in range(lines):
            y_recv(d, s).wait_recv()
            y_send(d, s).wait_send()
        for d in range(1, lines):
            z_send(d, s).wait_send()
        for one in c_recv(s):
            one.wait_recv()
        c_own(s).wait()
        for one in x_rest(s) + c_rest(s):
            one.wait_send()

        @pl.when(s < PIECES)
        def _():
            xv_send(s).wait_send()

    for one in listed:
        one.wait()


def gather(basis_t, diag, off, owners, tile_block):
    n_rows = lax.axis_size("rows")
    width, nodes = basis_t.shape
    rounds = 2 * PIECES
    kinds = (n_rows // 4 - 1) + n_rows // 4 + 8
    any_ = pl.BlockSpec(memory_space=pl.ANY)
    dma = pltpu.SemaphoreType.DMA
    return pl.pallas_call(
        functools.partial(gather_kernel, n_rows),
        out_shape=[
            jax.ShapeDtypeStruct((n_rows, width // 2, nodes), basis_t.dtype),
            jax.ShapeDtypeStruct(off.shape, off.dtype),
            jax.ShapeDtypeStruct(diag.shape, diag.dtype),
            jax.ShapeDtypeStruct(owners.shape, owners.dtype),
            jax.ShapeDtypeStruct(tile_block.shape, tile_block.dtype),
            jax.ShapeDtypeStruct((3, width, nodes), basis_t.dtype),
        ],
        in_specs=[any_] * 5,
        out_specs=[any_] * 6,
        scratch_shapes=[dma, dma((rounds, kinds)), dma((rounds, kinds)), dma((2,)), dma((2,))],
        compiler_params=pltpu.CompilerParams(collective_id=0, has_side_effects=True),
    )(basis_t, off, diag, owners, tile_block)


def project_kernel(groups, per_step, panel_counts, homes, *refs):
    n_panels = sum(panel_counts)
    lists = [refs[2 * g : 2 * g + 2] for g in range(groups)]
    vall = refs[2 * groups]
    blocks = [refs[2 * groups + 1 + 2 * g : 2 * groups + 3 + 2 * g] for g in range(groups)]
    start = 4 * groups + 1
    panels = refs[start : start + n_panels]
    out = refs[start + n_panels]
    step = pl.program_id(0)

    @pl.when(step == 0)
    def _():
        out[...] = jnp.zeros_like(out)

    done = 0
    for g in range(groups):
        (own, tile), (off, diag) = lists[g], blocks[g]
        images = []
        for i in range(per_step):
            b = step * per_step + i
            left = [
                vall[own[b, k], :, pl.ds(pl.multiple_of(tile[b, k] * BS, BS), BS)] for k in range(TPR)
            ] + [vall[homes[g], :, pl.ds(pl.multiple_of(b * BS, BS), BS)]]
            right = [off[i, k] for k in range(TPR)] + [diag[i]]
            images.append(
                lax.dot_general(
                    jnp.concatenate(left, axis=1),
                    jnp.concatenate(right, axis=1),
                    NT,
                    preferred_element_type=jnp.float32,
                ).astype(jnp.bfloat16)
            )
        image = jnp.concatenate(images, axis=1)
        row = 0
        for panel in panels[done : done + panel_counts[g]]:
            size = panel.shape[-2]
            values = panel[...].reshape(size, panel.shape[-1])
            out[pl.ds(row, size), :] += lax.dot_general(values, image, NT, preferred_element_type=jnp.float32)
            row += size
        done += panel_counts[g]


def project(homes, lists, vall, blocks, panels, per_step=4):
    groups = len(lists)
    local_rows = blocks[0][0].shape[0]
    total = sum(p.shape[-2] for p, _ in panels[0])
    smem = pl.BlockSpec(memory_space=pltpu.SMEM)
    span = per_step * BS
    args, specs = [homes], [smem]
    for pair in lists:
        args += pair
        specs += [smem, smem]
    args.append(vall)
    specs.append(pl.BlockSpec(vall.shape, lambda i: (0, 0, 0), pipeline_mode=pl.Buffered(1)))
    for off, diag in blocks:
        args += [off, diag]
        specs += [
            pl.BlockSpec((per_step, TPR, BS, BS), lambda i: (i, 0, 0, 0)),
            pl.BlockSpec((per_step, BS, BS), lambda i: (i, 0, 0)),
        ]
    for group in panels:
        for array, lead in group:
            args.append(array)
            if lead is None:
                specs.append(pl.BlockSpec((array.shape[0], span), lambda i: (0, i)))
            else:
                specs.append(pl.BlockSpec((1, array.shape[1], span), lambda i, lead=lead: (lead, 0, i)))
    width = vall.shape[1]
    return pl.pallas_call(
        functools.partial(project_kernel, groups, per_step, tuple(len(g) for g in panels)),
        out_shape=jax.ShapeDtypeStruct((total, width), jnp.float32),
        grid=(local_rows // per_step,),
        in_specs=specs,
        out_specs=pl.BlockSpec((total, width), lambda i: (0, 0)),
        compiler_params=pltpu.CompilerParams(vmem_limit_bytes=48 * MIB),
    )(*args)


def scatter_kernel(n_rows, partial, out, land, send, recv):
    r, c = lax.axis_index("rows"), lax.axis_index("cols")
    x = r % 2
    rows, width = out.shape[0], partial.shape[1]
    barrier = pltpu.get_barrier_semaphore()
    for d in range(1, n_rows):
        pl.semaphore_signal(barrier, inc=1, device_id=((r + d) % n_rows, c), device_id_type=MESH)
    pl.semaphore_wait(barrier, n_rows - 1)

    def share(target):
        per_half = n_rows // 2
        place = (target // per_half + c) % 2 * per_half + target % per_half
        return partial.at[pl.ds(pl.multiple_of(place * rows, rows), rows), :]

    def copy(d):
        target = (r + d) % n_rows
        return pltpu.make_async_remote_copy(
            src_ref=share(target), dst_ref=land.at[d], send_sem=send.at[d], recv_sem=recv.at[d],
            device_id=(target, c), device_id_type=MESH,
        )

    for d in range(1, n_rows):
        copy(d).start()
    mine = share(r)[...]
    other = jnp.zeros_like(mine)
    for d in range(1, n_rows):
        copy(d).wait_recv()
        if d % 2:
            other = other + land[d]
        else:
            mine = mine + land[d]
    first = x == 0
    out[:, pl.ds(0, width)] = jnp.where(first, mine, other)
    out[:, pl.ds(width, width)] = jnp.where(first, other, mine)
    for d in range(1, n_rows):
        copy(d).wait_send()


def scatter(partial):
    n_rows = lax.axis_size("rows")
    rows, width = partial.shape[0] // n_rows, partial.shape[1]
    dma = pltpu.SemaphoreType.DMA
    vmem = pl.BlockSpec(memory_space=pltpu.VMEM)
    return pl.pallas_call(
        functools.partial(scatter_kernel, n_rows),
        out_shape=jax.ShapeDtypeStruct((rows, 2 * width), jnp.float32),
        in_specs=[vmem],
        out_specs=vmem,
        scratch_shapes=[pltpu.VMEM((n_rows, rows, width), jnp.float32), dma((n_rows,)), dma((n_rows,))],
        compiler_params=pltpu.CompilerParams(collective_id=1, has_side_effects=True),
    )(partial)


def on_chip_pairs(basis_t, diag_tiles, off_tiles, owners, tile_block):
    vall, offp, diagp, ownp, tilep, pv = gather(basis_t, diag_tiles, off_tiles, owners, tile_block)
    r = lax.axis_index("rows")
    homes = jnp.stack([r, r + 1 - 2 * (r % 2)]).astype(jnp.int32)
    partial = project(
        homes,
        [(owners, tile_block), (ownp, tilep)],
        vall,
        [(off_tiles, diag_tiles), (offp, diagp)],
        [[(basis_t, None), (pv, 0)], [(pv, 1), (pv, 2)]],
    )
    return scatter(partial)


def general(basis_t, diag_tiles, off_tiles, owners, tile_block):
    vall = lax.all_gather(basis_t, "rows", axis=0, tiled=False)
    whole = lax.all_gather(basis_t, "cols", axis=0, tiled=True)
    homes = lax.axis_index("rows").astype(jnp.int32).reshape(1)
    partial = project(
        homes, [(owners, tile_block)], vall, [(off_tiles, diag_tiles)], [[(whole, None)]]
    )
    return lax.psum_scatter(partial, "rows", scatter_dimension=0, tiled=True)


def solution(mesh):
    in_specs = (
        P("cols", "rows"),
        P("rows", None, None),
        P("rows", None, None, None),
        P("rows", None),
        P("rows", None),
    )
    pairs = mesh.shape["cols"] == 2 and mesh.shape["rows"] % 4 == 0
    return jax.shard_map(
        on_chip_pairs if pairs else general,
        mesh=mesh, in_specs=in_specs, out_specs=P("rows", "cols"), check_vma=False,
    )
```

time: 522 us -> 288 us (0.55)
  waiting for transfers between devices: 432 us -> 0 us
  Pallas kernels: 0 us -> 280 us
  local copies, waits for them, and re-layouts: 58.5 us -> 7.61 us
  matrix products: 16.9 us -> 0 us
  between operations: 13.2 us -> 0.08 us
    all_gather x2 -> x0, waiting for transfers between devices: 353 us -> none  [the longest x1 353 us: per_device(): whole_basis = lax.all_gather(basis_t, 'rows', axis=1, tiled=True)]
    pallas_call x0 -> x3, Pallas kernels: none -> 280 us  [the longest x1 234 us: gather(): pl.pallas_call(functools.partial(gather_kernel, n_rows), out_shape=[jax.S...]
    reduce_scatter x1 -> x0, waiting for transfers between devices: 78.8 us -> none  [per_device(): lax.psum_scatter(partial_sums, 'rows', scatter_dimension=0, tiled=True)]
    reshape x1 -> x0, local copies, waits for them, and re-layouts: 40.5 us -> none  [per_device(): all_blocks = whole_basis.reshape(width, row_devices * local_rows, BS)]
    dot_general x3 -> x0, matrix products: 16.9 us -> none  [the longest x1 10.7 us: per_device(): jnp.einsum('cbkj,bkij->cbi', tile_panels, off_tiles, preferred_element_ty...]
    gather x1 -> x0, local copies, waits for them, and re-layouts: 12.7 us -> none  [per_device(): tile_panels = all_blocks[:, flat_owners * local_rows + flat_blocks, :]]
  transfers between devices with their start and end apart: 3 -> 0, of which waited for: 2 -> 0; matrix products, arithmetic and copies ran while one was open for 13% -> 0% of each run, Pallas kernels for 0% -> 0%
where the time goes in v1:
time: 288 us
  Pallas kernels  280 us (97%)
  local copies, waits for them, and re-layouts  7.61 us (3%)
    pallas_call x1, Pallas kernels, gather(): pl.pallas_call(functools.partial(gather_kernel, n_rows), out_shape=[jax.S...  234 us
    pallas_call x1, Pallas kernels, scatter(): pl.pallas_call(functools.partial(scatter_kernel, n_rows), out_shape=jax.S...  26.7 us
    pallas_call x1, Pallas kernels, project(): pl.pallas_call(functools.partial(project_kernel, groups, per_step, tuple(...  19 us
    unnamed x19, local copies, waits for them, and re-layouts  7.61 us

profile of v1, /device:TPU:0, one launch (start us, length us, event | category | flops | bytes accessed | tf_op | source)
XLA Modules:
  0.0 287.9 jit_solution(14021850837482804923)
XLA Ops:
  0.0 0.0 copy-start.1
  0.0 0.0 copy-start
  0.0 0.1 pad_add_fusion.homes
  0.1 1.5 copy.8.own.refs_0_
  1.6 0.0 copy-start.4
  1.6 1.4 copy.9.tile.refs_1_
  3.0 0.0 copy-start.5
  3.0 234.4 %shard_map.55 = (bf16[16,128,4096]{2,1,0:T(8,128)(2,1)}, bf16[32,8,128,128]{3,2,1,0:T(8,128)(2,1)}, bf16[32,128,128]{2,1,0:T(8,128)(2,1)}, s32[32,8]{1,0:T(8,128...) custom-call(bf16[256,4096]{1,0:T(8,128)(2,1)} %refs_9_.1, bf16[32,8,128,128]{3,2,1,0:T(8,128)(2,1)} %refs_5_.1, ...), custom_call_target="tpu_custom_call" | custom-call | tf_op jit(solution)/shard_map/pallas_call | solution.py:181
  237.3 0.0 copy-done.1
  237.4 0.0 copy-done
  237.4 0.0 copy-done.4
  237.4 0.0 copy-done.5
  237.4 0.0 copy-start.2
  237.4 1.2 copy-done.2
  238.6 0.0 copy-start.6
  238.6 0.7 copy-done.6
  239.3 0.0 copy-start.7
  239.3 0.7 copy-done.7
  240.1 19.0 %shard_map.56.partial = f32[512,128]{1,0:T(8,128)S(1)} custom-call(s32[2]{0:T(128)S(1)} %pad_add_fusion.homes, s32[32,8]{1,0:T(8,128)S(1)} %copy-done.4, s32[32,8]{1,0:T(8,128)S(1)} %copy-done.5, s32[32,8]{1,0:T(8,128)S(1)} %copy-done.6, s32[32,8]{1,0:T(8,128)S(1)} %copy-done.7, bf16[16,128,4096]{2,1,0:T(8,128)(2,1)} %get-tuple-element.13.refs_4_, ...), custom_call_target="tpu_custom_call" | custom-call | tf_op jit(solution)/shard_map/pallas_call | solution.py:266
  259.1 0.0 copy-start.3
  259.1 0.7 copy-done.3
  259.8 26.7 %shard_map.57 = f32[32,256]{1,0:T(8,128)} custom-call(f32[512,128]{1,0:T(8,128)} %copy-done.3), custom_call_target="tpu_custom_call" | custom-call | tf_op jit(solution)/shard_map/pallas_call | solution.py:319
  286.5 1.4 copy.11
Async XLA Ops:
  0.0 237.4 %copy-start.1 = (bf16[32,128,128]{2,1,0:T(8,128)(2,1)S(1)}, bf16[32,128,128]{2,1,0:T(8,128)(2,1)}, u32[]{:S(2)}) copy-start(bf16[32,128,128]{2,1,0:T(8,128)(2,1)} %refs_6_.1) | copy-start | bytes 3145732
  0.0 237.4 %copy-start = (bf16[256,4096]{1,0:T(8,128)(2,1)S(1)}, bf16[256,4096]{1,0:T(8,128)(2,1)}, u32[]{:S(2)}) copy-start(bf16[256,4096]{1,0:T(8,128)(2,1)} %refs_9_.1) | copy-start | bytes 6291460
  1.6 235.8 %copy-start.4 = (s32[32,8]{1,0:T(8,128)S(1)}, s32[32,8]{1,0:T(8,128)}, u32[]{:S(2)}) copy-start(s32[32,8]{1,0:T(8,128)} %copy.8.own.refs_0_) | copy-start | bytes 3076
  3.0 234.4 %copy-start.5 = (s32[32,8]{1,0:T(8,128)S(1)}, s32[32,8]{1,0:T(8,128)}, u32[]{:S(2)}) copy-start(s32[32,8]{1,0:T(8,128)} %copy.9.tile.refs_1_) | copy-start | bytes 3076
  237.4 1.2 copy-start.2
  238.6 0.7 copy-start.6
  239.3 0.7 copy-start.7
  259.1 0.7 copy-start.3

commit v2 on v1

v2 whole, which is shorter than its diff:
```python
import functools

import jax
import jax.numpy as jnp
from jax import lax
from jax.experimental import pallas as pl
from jax.experimental.pallas import tpu as pltpu
from jax.sharding import PartitionSpec as P

BS = 128
TPR = 8
LINE = 4
PIECES = 8
PIECE = 16
ROUNDS = 2 * PIECES
SWITCH = 13
KINDS = 16
FAMILY = 5
MESH = pl.DeviceIdType.MESH
NT = (((1,), (1,)), ((), ()))
MIB = 1 << 20


def START(copy):
    copy.start()


def WAIT_SEND(copy):
    copy.wait_send()


def gather_kernel(
    basis, off, diag, own, tile, vall, offp, diagp, ownp, tilep, pv0, pvx, pv2,
    local_sem, send, recv, bsend, brecv, isend, irecv,
):
    r, c = lax.axis_index("rows"), lax.axis_index("cols")
    x, y, z = r % 2, (r // 2) % 2, r // 4
    slab = basis.shape[0] // 2
    half_rows = off.shape[0] // 2
    side = r + 1 - 2 * x
    across = r + 2 - 4 * y
    twin = 1 - c
    FWD, Y0 = 4, 5
    XV, XA, XD, CA, CB, CD, CO = range(9, KINDS)

    barrier = pltpu.get_barrier_semaphore()
    friends = [(side, c), (across, c), (r, twin)] + [((r + 4 * d) % (4 * LINE), c) for d in range(1, LINE)]
    for friend in friends:
        pl.semaphore_signal(barrier, inc=1, device_id=friend, device_id_type=MESH)
    pl.semaphore_wait(barrier, len(friends))

    def remote(src, dst, ssem, rsem, device):
        return pltpu.make_async_remote_copy(
            src_ref=src, dst_ref=dst, send_sem=ssem, recv_sem=rsem, device_id=device, device_id_type=MESH
        )

    def copy(s, kind, src, dst, device):
        return remote(src, dst, send.at[s, kind], recv.at[s, kind], device)

    def band(ref, start):
        return ref.at[pl.ds(pl.multiple_of(start, PIECE), PIECE), :]

    def part(line, level, s):
        first = line * 4 + level * 2 + (x + s % 2) % 2
        return band(vall.at[first], (s // 2) * PIECE)

    def z_copy(family, s, target, origin, kind):
        here = part(origin, y if family == 0 else 1 - y, s)
        device = (target * 4 + r % 4, c)
        if family == 0:
            return copy_z(send.at[s, kind], recv.at[s, origin], here, device)
        return copy_z(bsend.at[s - SWITCH, kind], brecv.at[s - SWITCH, origin], here, device)

    def copy_z(ssem, rsem, here, device):
        return remote(here, here, ssem, rsem, device)

    def z_each(family, s, act):
        for t in range(LINE):
            near = (z != t) & (z - t <= 2) & (t - z <= 2)

            @pl.when(near)
            def _():
                act(z_copy(family, s, t, z, t))

    def z_forward(family, s, origin, act):
        if origin in (0, LINE - 1):
            @pl.when(z == (2 if origin == 0 else 1))
            def _():
                act(z_copy(family, s, LINE - 1 - origin, origin, FWD))

    def z_arrive(family, s, then):
        for o in range(LINE):
            @pl.when(z != o)
            def _():
                z_copy(family, s, (z + 1) % LINE, o, FWD).wait_recv()
                z_forward(family, s, o, START)
                then(o)

    def y_send(s, line):
        here = part(line, y, s)
        return copy(s, Y0 + line, here, here, (across, c))

    def y_recv(s, line):
        there = part(line, 1 - y, s)
        return copy(s, Y0 + line, there, there, (across, c))

    def xv_send(s):
        src = band(basis, (1 - x) * slab + s * PIECE)
        return copy(s, XV, src, band(vall.at[r], s * PIECE), (side, c))

    def xv_recv(s):
        dst = band(vall.at[side], s * PIECE)
        return copy(s, XV, dst, dst, (side, c))

    def xb(s):
        start = (s - PIECES) * PIECE
        return copy(s, XV, band(basis, x * slab + start), band(pvx, start), (side, c))

    def cb_vall(s):
        return copy(s, CB, band(vall.at[side], s * PIECE), band(pv2, x * slab + s * PIECE), (r, twin))

    def cb_rest(s):
        start = (s - PIECES) * PIECE
        return copy(s, CB, band(pvx, start), band(pv2, (1 - x) * slab + start), (r, twin))

    def x_tiles(s):
        at = c * half_rows + s
        return [
            copy(s, XA, off.at[at], offp.at[at], (side, c)),
            copy(s, XD, diag.at[at], diagp.at[at], (side, c)),
        ]

    def c_tiles(s, core):
        at = core * half_rows + s
        return [
            copy(s, CA, offp.at[at], offp.at[at], (r, twin)),
            copy(s, CD, diagp.at[at], diagp.at[at], (r, twin)),
        ]

    def c_own(s):
        return copy(s, CO, band(basis, s * PIECE), band(pv0, s * PIECE), (r, twin))

    keep = pltpu.make_async_copy(basis.at[pl.ds(pl.multiple_of(x * slab, slab), slab), :], vall.at[r], local_sem)
    keep.start()
    listed = [
        remote(a, b, isend.at[i], irecv.at[i], (side, c)) for i, (a, b) in enumerate(((own, ownp), (tile, tilep)))
    ]
    xv_send(0).start()
    for one in listed:
        one.start()
    keep.wait()

    def pass_on(s, late):
        def onward(o):
            if not late:
                y_send(s, o).start()

        z_arrive(0, s, onward)
        if late:
            z_arrive(1, s, lambda o: None)
        for came, go in zip(x_tiles(s), c_tiles(s, c)):
            came.wait_recv()
            go.start()

        @pl.when(s >= PIECES)
        def _():
            xb(s).wait_recv()
            cb_rest(s).start()

    def begin(s, late):
        @pl.when(s < PIECES - 1)
        def _():
            xv_send(s + 1).start()

        @pl.when((s >= 1) & (s <= PIECES))
        def _():
            xv_recv(s - 1).wait_recv()
            cb_vall(s - 1).start()

        if late:
            z_each(0, s, START)
            y_recv_late(s).wait_recv()
            z_each(1, s, START)
        else:
            z_each(0, s, START)
            y_send(s, z).start()

            @pl.when(s == PIECES + 1)
            def _():
                for later in range(SWITCH, ROUNDS):
                    y_send(later, z).start()
        for one in x_tiles(s):
            one.start()
        c_own(s).start()

        @pl.when(s >= PIECES)
        def _():
            xb(s).start()

    def y_recv_late(s):
        return y_recv(s, z)

    @pl.loop(0, SWITCH)
    def _(s):
        begin(s, False)

        @pl.when(s >= 1)
        def _():
            pass_on(s - 1, False)

    begin(SWITCH, True)
    pass_on(SWITCH - 1, False)

    @pl.loop(SWITCH + 1, ROUNDS)
    def _(s):
        begin(s, True)
        pass_on(s - 1, True)

    pass_on(ROUNDS - 1, True)

    @pl.loop(0, SWITCH)
    def _(s):
        for o in range(LINE):
            y_recv(s, o).wait_recv()
            y_send(s, o).wait_send()

    @pl.loop(SWITCH, ROUNDS)
    def _(s):
        y_send(s, z).wait_send()
        z_each(1, s, WAIT_SEND)
        for o in (0, LINE - 1):
            z_forward(1, s, o, WAIT_SEND)

    @pl.loop(0, ROUNDS)
    def _(s):
        z_each(0, s, WAIT_SEND)
        for o in (0, LINE - 1):
            z_forward(0, s, o, WAIT_SEND)
        for one in x_tiles(s) + c_tiles(s, c):
            one.wait_send()
        for one in c_tiles(s, twin):
            one.wait_recv()
        c_own(s).wait()

        @pl.when(s < PIECES)
        def _():
            xv_send(s).wait_send()
            cb_vall(s).wait()

        @pl.when(s >= PIECES)
        def _():
            xb(s).wait_send()
            cb_rest(s).wait()

    for one in listed:
        one.wait()


def gather(basis_t, diag, off, owners, tile_block):
    width, nodes = basis_t.shape
    any_ = pl.BlockSpec(memory_space=pl.ANY)
    dma = pltpu.SemaphoreType.DMA
    like = lambda a: jax.ShapeDtypeStruct(a.shape, a.dtype)
    return pl.pallas_call(
        gather_kernel,
        out_shape=[
            jax.ShapeDtypeStruct((4 * LINE, width // 2, nodes), basis_t.dtype),
            like(off), like(diag), like(owners), like(tile_block),
            like(basis_t),
            jax.ShapeDtypeStruct((width // 2, nodes), basis_t.dtype),
            like(basis_t),
        ],
        in_specs=[any_] * 5,
        out_specs=[any_] * 8,
        scratch_shapes=[
            dma, dma((ROUNDS, KINDS)), dma((ROUNDS, KINDS)),
            dma((ROUNDS - SWITCH, FAMILY)), dma((ROUNDS - SWITCH, FAMILY)), dma((2,)), dma((2,)),
        ],
        compiler_params=pltpu.CompilerParams(collective_id=0, has_side_effects=True),
    )(basis_t, off, diag, owners, tile_block)


def project_kernel(groups, per_step, panel_counts, homes, *refs):
    n_panels = sum(panel_counts)
    lists = [refs[2 * g : 2 * g + 2] for g in range(groups)]
    vall = refs[2 * groups]
    blocks = [refs[2 * groups + 1 + 2 * g : 2 * groups + 3 + 2 * g] for g in range(groups)]
    start = 4 * groups + 1
    panels = refs[start : start + n_panels]
    out = refs[start + n_panels]
    step = pl.program_id(0)

    @pl.when(step == 0)
    def _():
        out[...] = jnp.zeros_like(out)

    done = 0
    for g in range(groups):
        (own, tile), (off, diag) = lists[g], blocks[g]
        images = []
        for i in range(per_step):
            b = step * per_step + i
            left = [
                vall[own[b, k], :, pl.ds(pl.multiple_of(tile[b, k] * BS, BS), BS)] for k in range(TPR)
            ] + [vall[homes[g], :, pl.ds(pl.multiple_of(b * BS, BS), BS)]]
            right = [off[i, k] for k in range(TPR)] + [diag[i]]
            images.append(
                lax.dot_general(
                    jnp.concatenate(left, axis=1),
                    jnp.concatenate(right, axis=1),
                    NT,
                    preferred_element_type=jnp.float32,
                ).astype(jnp.bfloat16)
            )
        image = jnp.concatenate(images, axis=1)
        row = 0
        span = per_step * BS
        pieces = [p[...] for p in panels[done : done + panel_counts[g]]]
        starts = [None] * len(pieces)
        if g == 1:
            share = vall[homes[g], :, pl.ds(pl.multiple_of(step * span, span), span)]
            pieces = [share] + pieces
            size = share.shape[0]
            starts = [homes[2] * size, (1 - homes[2]) * size, 2 * size]
        for values, at in zip(pieces, starts):
            size = values.shape[0]
            place = pl.ds(row if at is None else pl.multiple_of(at, BS), size)
            out[place, :] += lax.dot_general(values, image, NT, preferred_element_type=jnp.float32)
            row += size
        done += panel_counts[g]


def project(homes, lists, vall, blocks, panels, per_step=4):
    groups = len(lists)
    local_rows = blocks[0][0].shape[0]
    total = sum(p.shape[0] for p in panels[0])
    smem = pl.BlockSpec(memory_space=pltpu.SMEM)
    span = per_step * BS
    args, specs = [homes], [smem]
    for pair in lists:
        args += pair
        specs += [smem, smem]
    args.append(vall)
    specs.append(pl.BlockSpec(vall.shape, lambda i: (0, 0, 0), pipeline_mode=pl.Buffered(1)))
    for off, diag in blocks:
        args += [off, diag]
        specs += [
            pl.BlockSpec((per_step, TPR, BS, BS), lambda i: (i, 0, 0, 0)),
            pl.BlockSpec((per_step, BS, BS), lambda i: (i, 0, 0)),
        ]
    for group in panels:
        for array in group:
            args.append(array)
            specs.append(pl.BlockSpec((array.shape[0], span), lambda i: (0, i)))
    width = vall.shape[1]
    return pl.pallas_call(
        functools.partial(project_kernel, groups, per_step, tuple(len(g) for g in panels)),
        out_shape=jax.ShapeDtypeStruct((total, width), jnp.float32),
        grid=(local_rows // per_step,),
        in_specs=specs,
        out_specs=pl.BlockSpec((total, width), lambda i: (0, 0)),
        compiler_params=pltpu.CompilerParams(vmem_limit_bytes=48 * MIB),
    )(*args)


def scatter_kernel(n_rows, partial, out, land, send, recv):
    r, c = lax.axis_index("rows"), lax.axis_index("cols")
    x = r % 2
    rows, width = out.shape[0], partial.shape[1]
    barrier = pltpu.get_barrier_semaphore()
    for d in range(1, n_rows):
        pl.semaphore_signal(barrier, inc=1, device_id=((r + d) % n_rows, c), device_id_type=MESH)
    pl.semaphore_wait(barrier, n_rows - 1)

    def share(target):
        per_half = n_rows // 2
        place = (target // per_half + c) % 2 * per_half + target % per_half
        return partial.at[pl.ds(pl.multiple_of(place * rows, rows), rows), :]

    def copy(d):
        target = (r + d) % n_rows
        return pltpu.make_async_remote_copy(
            src_ref=share(target), dst_ref=land.at[d], send_sem=send.at[d], recv_sem=recv.at[d],
            device_id=(target, c), device_id_type=MESH,
        )

    for d in range(1, n_rows):
        copy(d).start()
    mine = share(r)[...]
    other = jnp.zeros_like(mine)
    for d in range(1, n_rows):
        copy(d).wait_recv()
        if d % 2:
            other = other + land[d]
        else:
            mine = mine + land[d]
    first = x == 0
    out[:, pl.ds(0, width)] = jnp.where(first, mine, other)
    out[:, pl.ds(width, width)] = jnp.where(first, other, mine)
    for d in range(1, n_rows):
        copy(d).wait_send()


def scatter(partial):
    n_rows = lax.axis_size("rows")
    rows, width = partial.shape[0] // n_rows, partial.shape[1]
    dma = pltpu.SemaphoreType.DMA
    vmem = pl.BlockSpec(memory_space=pltpu.VMEM)
    return pl.pallas_call(
        functools.partial(scatter_kernel, n_rows),
        out_shape=jax.ShapeDtypeStruct((rows, 2 * width), jnp.float32),
        in_specs=[vmem],
        out_specs=vmem,
        scratch_shapes=[pltpu.VMEM((n_rows, rows, width), jnp.float32), dma((n_rows,)), dma((n_rows,))],
        compiler_params=pltpu.CompilerParams(collective_id=1, has_side_effects=True),
    )(partial)


def on_chip_pairs(basis_t, diag_tiles, off_tiles, owners, tile_block):
    vall, offp, diagp, ownp, tilep, pv0, pvx, pv2 = gather(basis_t, diag_tiles, off_tiles, owners, tile_block)
    r = lax.axis_index("rows")
    x = r % 2
    side = r + 1 - 2 * x
    homes = jnp.stack([r, side, x]).astype(jnp.int32)
    partial = project(
        homes,
        [(owners, tile_block), (ownp, tilep)],
        vall,
        [(off_tiles, diag_tiles), (offp, diagp)],
        [[basis_t, pv0], [pvx, pv2]],
    )
    return scatter(partial)


def general(basis_t, diag_tiles, off_tiles, owners, tile_block):
    vall = lax.all_gather(basis_t, "rows", axis=0, tiled=False)
    whole = lax.all_gather(basis_t, "cols", axis=0, tiled=True)
    homes = lax.axis_index("rows").astype(jnp.int32).reshape(1)
    partial = project(
        homes, [(owners, tile_block)], vall, [(off_tiles, diag_tiles)], [[whole]]
    )
    return lax.psum_scatter(partial, "rows", scatter_dimension=0, tiled=True)


def solution(mesh):
    in_specs = (
        P("cols", "rows"),
        P("rows", None, None),
        P("rows", None, None, None),
        P("rows", None),
        P("rows", None),
    )
    pairs = mesh.shape["cols"] == 2 and mesh.shape["rows"] == 4 * LINE
    return jax.shard_map(
        on_chip_pairs if pairs else general,
        mesh=mesh, in_specs=in_specs, out_specs=P("rows", "cols"), check_vma=False,
    )
```

time: 288 us -> 250 us (0.87)
  Pallas kernels: 280 us -> 239 us
    pallas_call x1, Pallas kernels: 234 us -> 210 us  [gather(): pl.pallas_call(gather_kernel, out_shape=[jax.ShapeDtypeStruct((4 * LINE,...]
    pallas_call x1, Pallas kernels: 26.7 us -> 10.3 us  [scatter(): pl.pallas_call(functools.partial(scatter_kernel, n_rows), out_shape=jax.S...]
    unnamed x19 -> x21, local copies, waits for them, and re-layouts: 7.61 us -> 8.85 us
where the time goes in v2:
time: 250 us; the launch traced here: 248 us
  Pallas kernels  239 us (96%)
  local copies, waits for them, and re-layouts  8.85 us (4%)
    pallas_call x1, Pallas kernels, gather(): pl.pallas_call(gather_kernel, out_shape=[jax.ShapeDtypeStruct((4 * LINE,...  210 us
    pallas_call x1, Pallas kernels, project(): pl.pallas_call(functools.partial(project_kernel, groups, per_step, tuple(...  19.2 us
    pallas_call x1, Pallas kernels, scatter(): pl.pallas_call(functools.partial(scatter_kernel, n_rows), out_shape=jax.S...  10.3 us
    unnamed x21, local copies, waits for them, and re-layouts  8.85 us

profile of v2, /device:TPU:0, one launch (start us, length us, event | category | flops | bytes accessed | tf_op | source)
XLA Modules:
  0.0 248.3 jit_solution(13775445541306538194)
XLA Ops:
  0.0 0.0 copy-start.1
  0.0 0.0 copy-start
  0.0 0.1 pad_add_fusion.homes
  0.1 1.5 copy.8.own.refs_0_
  1.6 0.0 copy-start.5
  1.6 1.4 copy.9.tile.refs_1_
  3.0 0.0 copy-start.6
  3.0 209.8 %shard_map.55 = (bf16[16,128,4096]{2,1,0:T(8,128)(2,1)}, bf16[32,8,128,128]{3,2,1,0:T(8,128)(2,1)}, bf16[32,128,128]{2,1,0:T(8,128)(2,1)}, s32[32,8]{1,0:T(8,128...) custom-call(bf16[256,4096]{1,0:T(8,128)(2,1)} %refs_9_.1, ...), custom_call_target="tpu_custom_call" | custom-call | tf_op jit(solution)/shard_map/pallas_call | solution.py:264
  212.7 0.0 copy-done.1
  212.8 0.0 copy-done
  212.8 0.0 copy-done.5
  212.8 0.0 copy-done.6
  212.8 0.0 copy-start.3
  212.8 1.2 copy-done.3
  214.0 0.0 copy-start.4
  214.0 1.2 copy-done.4
  215.2 0.0 copy-start.7
  215.2 0.7 copy-done.7
  216.0 0.7 copy-done.8
  216.7 19.2 %shard_map.56.partial = f32[512,128]{1,0:T(8,128)S(1)} custom-call(s32[3]{0:T(128)S(1)} %pad_add_fusion.homes, s32[32,8]{1,0:T(8,128)S(1)} %copy-done.5, s32[32,8]{1,0:T(8,128)S(1)} %copy-done.6, s32[32,8]{1,0:T(8,128)S(1)} %copy-done.7, s32[32,8]{1,0:T(8,128)S(1)} %copy-done.8, bf16[16,128,4096]{2,1,0:T(8,128)(2,1)} %get-tuple-element.15.refs_4_, ...), custom_call_target="tpu_custom_call" | custom-call | tf_op jit(solution)/shard_map/pallas_call | solution.py:356
  235.9 0.0 copy-start.2
  235.9 0.7 copy-done.2
  236.6 10.3 %shard_map.57 = f32[32,256]{1,0:T(8,128)} custom-call(f32[512,128]{1,0:T(8,128)} %copy-done.2), custom_call_target="tpu_custom_call" | custom-call | tf_op jit(solution)/shard_map/pallas_call | solution.py:409
  246.9 1.4 copy.11
  (1 shorter events, 0.0 us)
Async XLA Ops:
  0.0 212.8 %copy-start.1 = (bf16[32,128,128]{2,1,0:T(8,128)(2,1)S(1)}, bf16[32,128,128]{2,1,0:T(8,128)(2,1)}, u32[]{:S(2)}) copy-start(bf16[32,128,128]{2,1,0:T(8,128)(2,1)} %refs_6_.1) | copy-start | bytes 3145732
  0.0 212.8 %copy-start = (bf16[256,4096]{1,0:T(8,128)(2,1)S(1)}, bf16[256,4096]{1,0:T(8,128)(2,1)}, u32[]{:S(2)}) copy-start(bf16[256,4096]{1,0:T(8,128)(2,1)} %refs_9_.1) | copy-start | bytes 6291460
  1.6 211.2 %copy-start.5 = (s32[32,8]{1,0:T(8,128)S(1)}, s32[32,8]{1,0:T(8,128)}, u32[]{:S(2)}) copy-start(s32[32,8]{1,0:T(8,128)} %copy.8.own.refs_0_) | copy-start | bytes 3076
  3.0 209.8 %copy-start.6 = (s32[32,8]{1,0:T(8,128)S(1)}, s32[32,8]{1,0:T(8,128)}, u32[]{:S(2)}) copy-start(s32[32,8]{1,0:T(8,128)} %copy.9.tile.refs_1_) | copy-start | bytes 3076
  212.8 1.2 copy-start.3
  214.0 1.2 copy-start.4
  215.2 0.7 copy-start.7
  216.0 0.7 copy-start.8
  235.9 0.7 copy-start.2

commit v3 on v2

--- a/solution.py
+++ b/solution.py
@@ -14,8 +14,10 @@
 PIECE = 16
 ROUNDS = 2 * PIECES
 SWITCH = 13
+LAG = 2
 KINDS = 16
 FAMILY = 5
+PER_STEP = 8
 MESH = pl.DeviceIdType.MESH
 NT = (((1,), (1,)), ((), ()))
 MIB = 1 << 20
@@ -31,7 +33,7 @@
 
 def gather_kernel(
     basis, off, diag, own, tile, vall, offp, diagp, ownp, tilep, pv0, pvx, pv2,
-    local_sem, send, recv, bsend, brecv, isend, irecv,
+    stage, local_sem, send, recv, bsend, brecv, isend, irecv,
 ):
     r, c = lax.axis_index("rows"), lax.axis_index("cols")
     x, y, z = r % 2, (r // 2) % 2, r // 4
@@ -43,6 +45,10 @@
     FWD, Y0 = 4, 5
     XV, XA, XD, CA, CB, CD, CO = range(9, KINDS)
 
+    load = pltpu.make_async_copy(basis.at[pl.ds(pl.multiple_of(x * slab, slab), slab), :], stage, local_sem.at[0])
+    keep = pltpu.make_async_copy(stage, vall.at[r], local_sem.at[1])
+    load.start()
+
     barrier = pltpu.get_barrier_semaphore()
     friends = [(side, c), (across, c), (r, twin)] + [((r + 4 * d) % (4 * LINE), c) for d in range(1, LINE)]
     for friend in friends:
@@ -140,14 +146,14 @@
     def c_own(s):
         return copy(s, CO, band(basis, s * PIECE), band(pv0, s * PIECE), (r, twin))
 
-    keep = pltpu.make_async_copy(basis.at[pl.ds(pl.multiple_of(x * slab, slab), slab), :], vall.at[r], local_sem)
-    keep.start()
     listed = [
         remote(a, b, isend.at[i], irecv.at[i], (side, c)) for i, (a, b) in enumerate(((own, ownp), (tile, tilep)))
     ]
     xv_send(0).start()
     for one in listed:
         one.start()
+    load.wait()
+    keep.start()
     keep.wait()
 
     def pass_on(s, late):
@@ -204,19 +210,14 @@
     def _(s):
         begin(s, False)
 
-        @pl.when(s >= 1)
-        def _():
-            pass_on(s - 1, False)
-
-    begin(SWITCH, True)
-    pass_on(SWITCH - 1, False)
-
-    @pl.loop(SWITCH + 1, ROUNDS)
-    def _(s):
-        begin(s, True)
-        pass_on(s - 1, True)
-
-    pass_on(ROUNDS - 1, True)
+        @pl.when(s >= LAG)
+        def _():
+            pass_on(s - LAG, False)
+
+    for s in range(SWITCH, ROUNDS + LAG):
+        if s < ROUNDS:
+            begin(s, True)
+        pass_on(s - LAG, s - LAG >= SWITCH)
 
     @pl.loop(0, SWITCH)
     def _(s):
@@ -273,7 +274,7 @@
         in_specs=[any_] * 5,
         out_specs=[any_] * 8,
         scratch_shapes=[
-            dma, dma((ROUNDS, KINDS)), dma((ROUNDS, KINDS)),
+            pltpu.VMEM((width // 2, nodes), basis_t.dtype), dma((2,)), dma((ROUNDS, KINDS)), dma((ROUNDS, KINDS)),
             dma((ROUNDS - SWITCH, FAMILY)), dma((ROUNDS - SWITCH, FAMILY)), dma((2,)), dma((2,)),
         ],
         compiler_params=pltpu.CompilerParams(collective_id=0, has_side_effects=True),
@@ -330,7 +331,7 @@
         done += panel_counts[g]
 
 
-def project(homes, lists, vall, blocks, panels, per_step=4):
+def project(homes, lists, vall, blocks, panels, per_step=PER_STEP):
     groups = len(lists)
     local_rows = blocks[0][0].shape[0]
     total = sum(p.shape[0] for p in panels[0])

time: 250 us -> 216 us (0.86)
  Pallas kernels: 239 us -> 205 us
    pallas_call x1, Pallas kernels: 210 us -> 178 us  [gather(): pl.pallas_call(gather_kernel, out_shape=[jax.ShapeDtypeStruct((4 * LINE,...]
where the time goes in v3:
time: 216 us; the launch traced here: 214 us
  Pallas kernels  205 us (95%)
  local copies, waits for them, and re-layouts  8.85 us (4%)
    pallas_call x1, Pallas kernels, gather(): pl.pallas_call(gather_kernel, out_shape=[jax.ShapeDtypeStruct((4 * LINE,...  178 us
    pallas_call x1, Pallas kernels, project(): pl.pallas_call(functools.partial(project_kernel, groups, per_step, tuple(...  17.3 us
    pallas_call x1, Pallas kernels, scatter(): pl.pallas_call(functools.partial(scatter_kernel, n_rows), out_shape=jax.S...  9.58 us
    unnamed x21, local copies, waits for them, and re-layouts  8.85 us

profile of v3, /device:TPU:0, one launch (start us, length us, event | category | flops | bytes accessed | tf_op | source)
XLA Modules:
  0.0 213.9 jit_solution(3004927504021947512)
XLA Ops:
  0.0 0.0 copy-start
  0.0 0.1 pad_add_fusion.homes
  0.1 1.5 copy.8.own.refs_0_
  1.6 0.0 copy-start.5
  1.6 1.4 copy.9.tile.refs_1_
  3.0 0.0 copy-start.6
  3.0 178.0 %shard_map.55 = (bf16[16,128,4096]{2,1,0:T(8,128)(2,1)}, bf16[32,8,128,128]{3,2,1,0:T(8,128)(2,1)}, bf16[32,128,128]{2,1,0:T(8,128)(2,1)}, s32[32,8]{1,0:T(8,128...) custom-call(bf16[256,4096]{1,0:T(8,128)(2,1)} %refs_9_.1, ...), custom_call_target="tpu_custom_call" | custom-call | tf_op jit(solution)/shard_map/pallas_call | solution.py:265
  181.0 0.0 copy-done.1
  181.0 0.0 copy-done
  181.0 0.0 copy-done.5
  181.0 0.0 copy-done.6
  181.0 0.0 copy-start.3
  181.0 1.2 copy-done.3
  182.2 0.0 copy-start.4
  182.2 1.2 copy-done.4
  183.4 0.0 copy-start.7
  183.4 0.7 copy-done.7
  184.2 0.0 copy-start.8
  184.2 0.7 copy-done.8
  184.9 17.3 %shard_map.56.partial = f32[512,128]{1,0:T(8,128)S(1)} custom-call(s32[3]{0:T(128)S(1)} %pad_add_fusion.homes, s32[32,8]{1,0:T(8,128)S(1)} %copy-done.5, s32[32,8]{1,0:T(8,128)S(1)} %copy-done.6, s32[32,8]{1,0:T(8,128)S(1)} %copy-done.7, s32[32,8]{1,0:T(8,128)S(1)} %copy-done.8, bf16[16,128,4096]{2,1,0:T(8,128)(2,1)} %get-tuple-element.15.refs_4_, ...), custom_call_target="tpu_custom_call" | custom-call | tf_op jit(solution)/shard_map/pallas_call | solution.py:357
  202.2 0.0 copy-start.2
  202.2 0.7 copy-done.2
  202.9 9.6 %shard_map.57 = f32[32,256]{1,0:T(8,128)} custom-call(f32[512,128]{1,0:T(8,128)} %copy-done.2), custom_call_target="tpu_custom_call" | custom-call | tf_op jit(solution)/shard_map/pallas_call | solution.py:410
  212.5 1.4 copy.11
  (1 shorter events, 0.0 us)
Async XLA Ops:
  0.0 181.0 %copy-start.1 = (bf16[32,128,128]{2,1,0:T(8,128)(2,1)S(1)}, bf16[32,128,128]{2,1,0:T(8,128)(2,1)}, u32[]{:S(2)}) copy-start(bf16[32,128,128]{2,1,0:T(8,128)(2,1)} %refs_6_.1) | copy-start | bytes 3145732
  0.0 181.0 %copy-start = (bf16[256,4096]{1,0:T(8,128)(2,1)S(1)}, bf16[256,4096]{1,0:T(8,128)(2,1)}, u32[]{:S(2)}) copy-start(bf16[256,4096]{1,0:T(8,128)(2,1)} %refs_9_.1) | copy-start | bytes 6291460
  1.6 179.4 %copy-start.5 = (s32[32,8]{1,0:T(8,128)S(1)}, s32[32,8]{1,0:T(8,128)}, u32[]{:S(2)}) copy-start(s32[32,8]{1,0:T(8,128)} %copy.8.own.refs_0_) | copy-start | bytes 3076
  3.0 178.0 %copy-start.6 = (s32[32,8]{1,0:T(8,128)S(1)}, s32[32,8]{1,0:T(8,128)}, u32[]{:S(2)}) copy-start(s32[32,8]{1,0:T(8,128)} %copy.9.tile.refs_1_) | copy-start | bytes 3076
  181.0 1.2 copy-start.3
  182.2 1.2 copy-start.4
  183.4 0.7 copy-start.7
  184.2 0.7 copy-start.8
  202.2 0.7 copy-start.2
